TPU v7x, 32 devices: a whole 2x2x4 slice. The times are simulated.
32 devices in a mesh: pipe: 4 (over x, core), dp: 2 (over y), vocab: 4 (over z).
Axes of the slice: x: 2, y: 2, z: 4, core: 2. Of those that a mesh axis runs over, the one named last changes fastest.
Arguments:
- hidden: bfloat16 [512, 4608], P(('pipe', 'dp', 'vocab')), may hold values from -6 to 6
- targets: int32 [512], P(('pipe', 'dp', 'vocab')), may hold values from 0 to 12287, as said below
- input_ids: int32 [512], P(('pipe', 'dp', 'vocab')), may hold values from 0 to 12287, as said below
- input_grads: bfloat16 [512, 4608], P(('pipe', 'dp', 'vocab')), may hold values from -0.3125 to 0.3125
- table: bfloat16 [12288, 4608], P(('pipe', 'vocab'), 'dp'), may hold values from -0.75 to 0.75
- keep: int32 [12288], P(('pipe', 'vocab')), may hold values from 0 to 1
- first_moment: bfloat16 [12288, 4608], P(('pipe', 'vocab'), 'dp'), may hold values from -0.015625 to 0.015625
- second_moment: bfloat16 [12288, 4608], P(('pipe', 'vocab'), 'dp'), may hold values from 9.983778e-07 to 9.953976e-06
Outputs:
- new_table: bfloat16 [12288, 4608], P(('pipe', 'vocab'), 'dp')
- new_first: bfloat16 [12288, 4608], P(('pipe', 'vocab'), 'dp')
- new_second: bfloat16 [12288, 4608], P(('pipe', 'vocab'), 'dp')
- loss: float32 [], replicated
Inputs may be any that keep to these rules, and one draw needn't show every extreme that they name: `targets`: names only rows with keep = 1. `input_ids`: names only rows with keep = 1.
All inputs are finite; a program needn't handle non-finite values.
Results may differ from a plain program's by a relative error of at most 0.0036.
Values may be sent and summed in bfloat16 or wider, within the bound.
A program may use at most 192 MiB of HBM per device.

v0:
```python
import math

import jax
import jax.numpy as jnp
from jax import lax
from jax.sharding import PartitionSpec as P

SOFTCAP = 30.0
LEARN = 0.01
EPSILON = 1e-08


def contract_last(left, right):
    return lax.dot_general(
        left, right, (((1,), (1,)), ((), ())), preferred_element_type=jnp.float32
    )


def contract_first(left, right):
    return lax.dot_general(
        left, right, (((0,), (0,)), ((), ())), preferred_element_type=jnp.float32
    )


def body(hidden, targets, input_ids, input_grads, table, keep, first_moment, second_moment):
    rows_here = table.shape[0]
    row_start = lax.axis_index(("pipe", "vocab")) * rows_here
    keepf = keep.astype(jnp.float32)
    scale = math.sqrt(hidden.shape[1])
    groups_dp = lax.axis_size("dp")
    row_iota = jnp.arange(rows_here, dtype=jnp.int32)
    partial_value = None
    finished = None
    paired = jnp.tile(targets[:, None], (1, groups_dp))
    halves, goal_pairs = (
        lax.all_to_all(hidden, "dp", split_axis=1, concat_axis=0, tiled=True),
        lax.all_to_all(paired, "dp", split_axis=1, concat_axis=0, tiled=True),
    )
    tokens_all, goal_cols = (
        lax.all_gather(halves, ("pipe", "vocab"), axis=0, tiled=True),
        lax.all_gather(goal_pairs, ("pipe", "vocab"), axis=0, tiled=True),
    )
    goals = goal_cols.reshape(-1)
    raw = lax.psum(contract_last(tokens_all, table), "dp")
    capped = SOFTCAP * jnp.tanh(raw / SOFTCAP)
    onehot = ((goals - row_start)[:, None] == row_iota[None, :]).astype(jnp.float32)
    weights = jnp.exp(capped) * keepf[None, :]
    local_total = jnp.sum(weights, axis=1)
    local_target = jnp.sum(capped * onehot, axis=1)
    total, target_logit = lax.psum((local_total, local_target), ("pipe", "vocab"))
    token_loss = jnp.sum(jnp.log(total) - target_logit)
    slope = 1.0 - (capped / SOFTCAP) ** 2
    dlogits = ((weights / total[:, None] - onehot) * slope).astype(jnp.bfloat16)
    head_term = contract_first(dlogits, tokens_all)
    finished = head_term
    ids_piece = lax.all_gather(input_ids, ("pipe", "vocab"), axis=0, tiled=True)
    grads_piece = lax.all_gather(input_grads, ("pipe", "vocab"), axis=0, tiled=True)
    selector = ((ids_piece - row_start)[None, :] == row_iota[:, None]).astype(jnp.bfloat16)
    gathered = jnp.dot(selector, grads_piece, preferred_element_type=jnp.float32)
    input_term = scale * gathered
    partial_value = input_term
    reduced = lax.psum_scatter(partial_value, "dp", scatter_dimension=1, tiled=True)
    finished = finished + reduced
    kept = keep[:, None] > 0
    first_new = (0.9 * first_moment.astype(jnp.float32) + 0.1 * finished).astype(jnp.bfloat16)
    second_new = (0.95 * second_moment.astype(jnp.float32) + 0.05 * finished * finished).astype(
        jnp.bfloat16
    )
    corr_one = 1.0 - 0.9**10
    corr_two = 1.0 - 0.95**10
    update = (
        first_new.astype(jnp.float32)
        / corr_one
        / (jnp.sqrt(second_new.astype(jnp.float32) / corr_two) + EPSILON)
    )
    table_new = (table.astype(jnp.float32) - LEARN * update).astype(jnp.bfloat16)
    new_table = jnp.where(kept, table_new, table)
    new_first = jnp.where(kept, first_new, first_moment)
    new_second = jnp.where(kept, second_new, second_moment)
    return (new_table, new_first, new_second, token_loss)


def solution(mesh):
    placed = (
        P(("pipe", "dp", "vocab"), None),
        P(("pipe", "dp", "vocab")),
        P(("pipe", "dp", "vocab")),
        P(("pipe", "dp", "vocab"), None),
        P(("pipe", "vocab"), "dp"),
        P(("pipe", "vocab")),
        P(("pipe", "vocab"), "dp"),
        P(("pipe", "vocab"), "dp"),
    )
    return jax.shard_map(
        body,
        mesh=mesh,
        in_specs=placed,
        out_specs=(
            P(("pipe", "vocab"), "dp"),
            P(("pipe", "vocab"), "dp"),
            P(("pipe", "vocab"), "dp"),
            P(),
        ),
        check_vma=False,
    )
```

profile of v0, /device:TPU:0, one launch (start us, length us, event | category | flops | bytes accessed | tf_op | source)
XLA Modules:
  0.0 346.2 jit_solution(7954604429281435240)
XLA Ops:
  7.2 0.0 all-gather.3.cloned.1.call-start
  7.2 0.9 copy.16
  8.1 8.7 %all_to_all.35 = bf16[16,2,2304]{2,0,1:T(8,128)(2,1)} all-to-all(bf16[16,2,2304]{2,0,1:T(8,128)(2,1)S(1)} %bitcast.16), channel_id=1, replica_groups=mesh['pipe'=4,'dp'=2,'vocab'=4] {'dp'}, dimensions={1} | all-to-all | bytes 294912 | tf_op jit(solution)/shard_map/all_to_all | solution.py:36
  16.8 0.0 all-gather.3.cloned.1.call-update
  16.9 0.0 all-gather.5.cloned.1.call-start
  16.9 0.7 all-gather.5.cloned.1.call-update
  17.6 0.0 copy-start.2
  17.6 0.0 copy-start.4
  17.6 0.0 copy-start.3
  17.6 0.0 all-reduce.6.cloned.1.call-start
  17.7 42.2 %all-gather.3.cloned.1.call-done = bf16[512,2304]{1,0:T(8,128)(2,1)} async-done(((bf16[32,2304]{1,0:T(8,128)(2,1)}), bf16[512,2304]{1,0:T(8,128)(2,1)}) %all-gather.3.cloned.1.call-update) | async-done | bytes 2359312 | tf_op jit(solution)/shard_map/all_gather | solution.py:40
  59.9 5.9 %fusion.14 = f32[512,768]{1,0:T(8,128)} fusion(bf16[512,2304]{1,0:T(8,128)(2,1)} %all-gather.3.cloned.1.call-done, bf16[768,2304]{1,0:T(8,128)(2,1)} %param.12), kind=kOutput, calls=%fused_computation.33 | convolution fusion | flops 1811939328 | bytes 7471104 | tf_op jit(solution)/shard_map/dot_general | solution.py:14
  65.8 0.0 all-reduce.6.cloned.1.call-update
  65.8 0.0 copy-done.2
  65.8 0.6 tile.2
  66.4 3.2 all-to-all-start.1
  69.6 0.0 reduce-scatter.2.cloned.1.call-start
  69.7 0.0 copy-done.4
  69.7 0.6 dynamic-slice
  71.6 0.0 copy-done.3
  71.6 0.2 dynamic-update-slice.1
  71.8 1.4 all-to-all-done.1
  73.3 0.1 reshape.27
  73.4 0.2 dynamic-update-slice
  73.5 9.1 %all-reduce.2 = (s32[256]{0:T(256)S(1)}, s32[512]{0:T(512)S(1)}) all-reduce(s32[256]{0:T(256)S(1)} %dynamic-update-slice.1, s32[512]{0:T(512)S(1)} %dynamic-update-slice), channel_id=1, replica_groups=mesh['pipe'=4,'dp'=2,'vocab'=4] {'pipe','vocab'}, use_global_device_ids=true, to_apply=%add.1 | all-reduce | flops 768 | bytes 6144
  82.7 20.6 %all-gather.5.cloned.1.call-done = bf16[256,4608]{1,0:T(8,128)(2,1)} async-done(((bf16[16,4608]{1,0:T(8,128)(2,1)}), bf16[256,4608]{1,0:T(8,128)(2,1)}) %all-gather.5.cloned.1.call-update) | async-done | bytes 2359312 | tf_op jit(solution)/shard_map/all_gather | solution.py:57
  103.3 8.9 %convolution_multiply_fusion = f32[768,4608]{1,0:T(8,128)} fusion(bf16[256,4608]{1,0:T(8,128)(2,1)} %all-gather.5.cloned.1.call-done, s32[256]{0:T(256)S(1)} %broadcast_subtract_fusion.1), kind=kOutput, calls=%fused_computation.1 | convolution fusion | flops 1815674880 | bytes 16516096 | tf_op jit(solution)/shard_map/dot_general | solution.py:59
  112.2 0.0 copy-start
  112.2 0.0 copy-start.1
  112.2 0.0 reduce-scatter.2.cloned.1.call-update
  112.2 0.7 copy-done
  112.9 43.6 %all-reduce.6.cloned.1.call-done = f32[512,768]{1,0:T(8,128)} async-done(((f32[512,768]{1,0:T(8,128)}), f32[512,768]{1,0:T(8,128)}) %all-reduce.6.cloned.1.call-update) | async-done | bytes 1572880 | tf_op jit(solution)/shard_map/psum | solution.py:44
  156.5 2.1 select_reduce_fusion
  158.6 33.4 %all-reduce.3 = (f32[512]{0:T(512)S(1)}, f32[512]{0:T(512)S(1)}) all-reduce(f32[512]{0:T(512)S(1)} %get-tuple-element.5, f32[512]{0:T(512)S(1)} %get-tuple-element.4), channel_id=1, replica_groups=mesh['pipe'=4,'dp'=2,'vocab'=4] {'pipe','vocab'}, use_global_device_ids=true, to_apply=%region_2.0 | all-reduce | flops 1024 | bytes 8192 | tf_op jit(solution)/shard_map/psum | solution.py:50
  192.0 0.6 subtract_reduce_fusion
  192.6 127.7 %reduce-scatter.2.cloned.1.call-done = f32[768,2304]{1,0:T(8,128)} async-done(((f32[768,4608]{1,0:T(8,128)}), f32[768,2304]{1,0:T(8,128)}) %reduce-scatter.2.cloned.1.call-update) | async-done | bytes 7077904 | tf_op jit(solution)/shard_map/reduce_scatter | solution.py:62
  320.2 0.0 copy-done.1
  320.2 19.5 %broadcast_select_fusion = (bf16[768,2304]{1,0:T(8,128)(2,1)}, bf16[768,2304]{1,0:T(8,128)(2,1)}, bf16[768,2304]{1,0:T(8,128)(2,1)}) fusion(bf16[768,2304]{1,0:T(8,128)(2,1)} %param.15, pred[768]{0:T(1024)(128)(4,1)S(1)} %broadcast_compare_fusion, bf16[768,2304]{1,0:T(8,128)(2,1)} %param.12, bf16[768,2304]{1,0:T(8,128)(2,1)} %param.14, ...), kind=kOutput, calls=%fused_computation.8 | convolution fusion | flops 1860501504 | bytes 32251648 | tf_op jit(solution)/shard_map/dot_general | solution.py:20
  (7 shorter events, 0.0 us)
Async XLA Ops:
  7.2 52.8 %all-gather.3.cloned.1.call-start = ((), (), s32[]{:S(2)}) async-start(), calls=%async_computation.3 | async-start | bytes 2506752 | tf_op jit(solution)/shard_map/all_gather | solution.py:40
  16.9 86.5 %all-gather.5.cloned.1.call-start = ((), (), s32[]{:S(2)}) async-start(), calls=%async_computation.5 | async-start | bytes 2506752 | tf_op jit(solution)/shard_map/all_gather | solution.py:57
  17.6 48.2 %copy-start.2 = (s32[16]{0:T(128)S(1)}, s32[16]{0:T(128)}, u32[]{:S(2)}) copy-start(s32[16]{0:T(128)} %param.9) | copy-start | bytes 196
  17.6 52.0 %copy-start.4 = (u32[32]{0:T(128)S(1)}, u32[32]{0:T(128)}, u32[]{:S(2)}) copy-start(u32[32]{0:T(128)} %constant.50) | copy-start | bytes 388
  17.6 53.9 %copy-start.3 = (s32[16]{0:T(128)S(1)}, s32[16]{0:T(128)}, u32[]{:S(2)}) copy-start(s32[16]{0:T(128)} %param.10) | copy-start | bytes 196
  17.6 138.8 %all-reduce.6.cloned.1.call-start = ((), (), s32[]{:S(2)}) async-start(), calls=%async_computation.4 | async-start | bytes 3145728 | tf_op jit(solution)/shard_map/psum | solution.py:44
  66.4 6.9 %all-to-all-start.1 = ((s32[16,2,1]{0,2,1:T(1,128)}), s32[16,2,1]{0,2,1:T(1,128)S(1)}, u32[]{:S(2)}, u32[]{:S(2)}) async-start(s32[16,2,1]{0,2,1:T(1,128)} %tile.2), calls=%async_computation.1 | async-start | bytes 2048 | tf_op jit(solution)/shard_map/all_to_all | solution.py:37
  69.6 250.6 %reduce-scatter.2.cloned.1.call-start = ((), (), s32[]{:S(2)}) async-start(), calls=%async_computation.6 | async-start | bytes 21233664 | tf_op jit(solution)/shard_map/reduce_scatter | solution.py:62
  112.2 0.7 copy-start
  112.2 208.1 %copy-start.1 = (bf16[512,2304]{1,0:T(8,128)(2,1)S(1)}, bf16[512,2304]{1,0:T(8,128)(2,1)}, u32[]{:S(2)}) copy-start(bf16[512,2304]{1,0:T(8,128)(2,1)} %all-gather.3.cloned.1.call-done) | copy-start | bytes 7077892
Sparse Core Ops, SparseCore 0:
  17.0 42.8 all-gather.2
  62.2 41.0 all-gather.4
  106.2 50.2 all-reduce.5
  158.7 161.4 reduce-scatter.1
where the time goes:
time: 347 us; the launch traced here: 346 us
  waiting for transfers between devices  236 us (68%)
  blocking collectives  51.2 us (15%)
  matrix products  34.2 us (10%)
  between operations  15.2 us (4%)
    reduce_scatter x1, waiting for transfers between devices, body(): lax.psum_scatter(partial_value, 'dp', scatter_dimension=1, tiled=True)  128 us
    psum x1, waiting for transfers between devices, body(): raw = lax.psum(contract_last(tokens_all, table), 'dp')  43.6 us
    all_gather x1, waiting for transfers between devices, body(): lax.all_gather(halves, ('pipe', 'vocab'), axis=0, tiled=True)  42.2 us
    psum x1, blocking collectives, body(): lax.psum((local_total, local_target), ('pipe', 'vocab'))  33.4 us
    all_gather x1, waiting for transfers between devices, body(): lax.all_gather(input_grads, ('pipe', 'vocab'), axis=0, tiled=True)  20.6 us
    dot_general x1, matrix products, contract_first(): lax.dot_general(left, right, (((0,), (0,)), ((), ())), preferred_element_...  19.5 us
    unnamed x1, blocking collectives  9.13 us
    dot_general x1, matrix products, body(): jnp.dot(selector, grads_piece, preferred_element_type=jnp.float32)  8.87 us
  transfers between devices with their start and end apart: 5, of which 5 were waited for; matrix products, arithmetic and copies ran while one was open for 6% of the time, Pallas kernels for 0%

commit v1 on v0

--- a/solution.py
+++ b/solution.py
@@ -29,38 +29,35 @@
     scale = math.sqrt(hidden.shape[1])
     groups_dp = lax.axis_size("dp")
     row_iota = jnp.arange(rows_here, dtype=jnp.int32)
-    partial_value = None
-    finished = None
-    paired = jnp.tile(targets[:, None], (1, groups_dp))
-    halves, goal_pairs = (
-        lax.all_to_all(hidden, "dp", split_axis=1, concat_axis=0, tiled=True),
-        lax.all_to_all(paired, "dp", split_axis=1, concat_axis=0, tiled=True),
+    both = jnp.stack([targets, input_ids])
+    packed = lax.all_to_all(
+        jnp.stack([hidden, input_grads]), "dp", split_axis=2, concat_axis=1, tiled=True
     )
-    tokens_all, goal_cols = (
-        lax.all_gather(halves, ("pipe", "vocab"), axis=0, tiled=True),
-        lax.all_gather(goal_pairs, ("pipe", "vocab"), axis=0, tiled=True),
+    ids_all = lax.all_gather(both, ("pipe", "vocab", "dp"), axis=1, tiled=True)
+    tokens_all = lax.all_gather(packed[0], ("pipe", "vocab"), axis=0, tiled=True)
+    grads_all = lax.all_gather(packed[1], ("pipe", "vocab"), axis=0, tiled=True)
+    tokens = tokens_all.shape[0]
+    share = tokens // groups_dp
+    start = lax.axis_index("dp") * share
+    goals = lax.dynamic_slice(ids_all[0], (start,), (share,))
+    raw = lax.psum_scatter(
+        contract_last(tokens_all, table), "dp", scatter_dimension=0, tiled=True
     )
-    goals = goal_cols.reshape(-1)
-    raw = lax.psum(contract_last(tokens_all, table), "dp")
     capped = SOFTCAP * jnp.tanh(raw / SOFTCAP)
     onehot = ((goals - row_start)[:, None] == row_iota[None, :]).astype(jnp.float32)
     weights = jnp.exp(capped) * keepf[None, :]
-    local_total = jnp.sum(weights, axis=1)
-    local_target = jnp.sum(capped * onehot, axis=1)
-    total, target_logit = lax.psum((local_total, local_target), ("pipe", "vocab"))
-    token_loss = jnp.sum(jnp.log(total) - target_logit)
+    local = jnp.stack([jnp.sum(weights, axis=1), jnp.sum(capped * onehot, axis=1)])
+    placed = lax.dynamic_update_slice(jnp.zeros((2, tokens), jnp.float32), local, (0, start))
+    sums = lax.psum(placed, ("pipe", "dp", "vocab"))
+    token_loss = jnp.sum(jnp.log(sums[0]) - sums[1])
+    total = lax.dynamic_slice(sums[0], (start,), (share,))
     slope = 1.0 - (capped / SOFTCAP) ** 2
     dlogits = ((weights / total[:, None] - onehot) * slope).astype(jnp.bfloat16)
-    head_term = contract_first(dlogits, tokens_all)
-    finished = head_term
-    ids_piece = lax.all_gather(input_ids, ("pipe", "vocab"), axis=0, tiled=True)
-    grads_piece = lax.all_gather(input_grads, ("pipe", "vocab"), axis=0, tiled=True)
-    selector = ((ids_piece - row_start)[None, :] == row_iota[:, None]).astype(jnp.bfloat16)
-    gathered = jnp.dot(selector, grads_piece, preferred_element_type=jnp.float32)
-    input_term = scale * gathered
-    partial_value = input_term
-    reduced = lax.psum_scatter(partial_value, "dp", scatter_dimension=1, tiled=True)
-    finished = finished + reduced
+    dlogits = lax.all_gather(dlogits, "dp", axis=0, tiled=True)
+    selector = ((ids_all[1] - row_start)[None, :] == row_iota[:, None]).astype(jnp.bfloat16)
+    finished = contract_first(dlogits, tokens_all) + scale * jnp.dot(
+        selector, grads_all, preferred_element_type=jnp.float32
+    )
     kept = keep[:, None] > 0
     first_new = (0.9 * first_moment.astype(jnp.float32) + 0.1 * finished).astype(jnp.bfloat16)
     second_new = (0.95 * second_moment.astype(jnp.float32) + 0.05 * finished * finished).astype(

time: 347 us -> 228 us (0.66)
  waiting for transfers between devices: 236 us -> 42.8 us
  blocking collectives: 51.2 us -> 124 us
  local copies, waits for them, and re-layouts: 3.29 us -> 10.4 us
    reduce_scatter x1, waiting for transfers between devices: 128 us -> 0.02 us  [body(): lax.psum_scatter(contract_last(tokens_all, table), 'dp', scatter_dimensio...]
    all_gather x0 -> x2, blocking collectives: none -> 77.6 us  [the longest x1 66.4 us: body(): ids_all = lax.all_gather(both, ('pipe', 'vocab', 'dp'), axis=1, tiled=True)]
    psum x1 -> x0, waiting for transfers between devices: 43.6 us -> none  [body(): raw = lax.psum(contract_last(tokens_all, table), 'dp')]
    all_gather x2, waiting for transfers between devices: 62.9 us -> 42.7 us  [the longest x1 42.7 us: body(): lax.all_gather(packed[0], ('pipe', 'vocab'), axis=0, tiled=True)]
    dot_general x1, matrix products: 19.5 us -> 4.95 us  [contract_first(): lax.dot_general(left, right, (((0,), (0,)), ((), ())), preferred_element_...]
    dot_general x1, matrix products: 8.87 us -> 20.3 us  [body(): jnp.dot(selector, grads_all, preferred_element_type=jnp.float32)]
    unnamed x1 -> x0, blocking collectives: 9.13 us -> none
    psum x1, blocking collectives: 33.4 us -> 36.9 us  [body(): sums = lax.psum(placed, ('pipe', 'dp', 'vocab'))]
  transfers between devices with their start and end apart: 5 -> 3, of which waited for: 5 -> 1; matrix products, arithmetic and copies ran while one was open for 6% -> 4% of each run, Pallas kernels for 0% -> 0%
where the time goes in v1:
time: 228 us; the launch traced here: 227 us
  blocking collectives  124 us (54%)
  waiting for transfers between devices  42.8 us (19%)
  matrix products  31.1 us (14%)
  between operations  13.9 us (6%)
  local copies, waits for them, and re-layouts  10.4 us (5%)
  other arithmetic  4.81 us (2%)
    all_gather x1, blocking collectives, body(): ids_all = lax.all_gather(both, ('pipe', 'vocab', 'dp'), axis=1, tiled=True)  66.4 us
    all_gather x1, waiting for transfers between devices, body(): lax.all_gather(packed[0], ('pipe', 'vocab'), axis=0, tiled=True)  42.7 us
    psum x1, blocking collectives, body(): sums = lax.psum(placed, ('pipe', 'dp', 'vocab'))  36.9 us
    dot_general x1, matrix products, body(): jnp.dot(selector, grads_all, preferred_element_type=jnp.float32)  20.3 us
    all_gather x1, blocking collectives, body(): dlogits = lax.all_gather(dlogits, 'dp', axis=0, tiled=True)  11.2 us
    all_to_all x1, blocking collectives, body(): lax.all_to_all(jnp.stack([hidden, input_grads]), 'dp', split_axis=2, conc...  9.55 us
    dot_general x1, matrix products, contract_last(): lax.dot_general(left, right, (((1,), (1,)), ((), ())), preferred_element_...  5.87 us
    dot_general x1, matrix products, contract_first(): lax.dot_general(left, right, (((0,), (0,)), ((), ())), preferred_element_...  4.95 us
  transfers between devices with their start and end apart: 3, of which 1 were waited for; matrix products, arithmetic and copies ran while one was open for 4% of the time, Pallas kernels for 0%

profile of v1, /device:TPU:0, one launch (start us, length us, event | category | flops | bytes accessed | tf_op | source)
XLA Modules:
  0.0 227.1 jit_solution(489731304706484116)
XLA Ops:
  7.2 0.0 all-gather.4.cloned.1.call-start
  7.2 1.0 pad_maximum_fusion
  8.2 3.0 %copy.27 = bf16[2,16,4608]{1,0,2:T(2,128)(2,1)S(1)} copy(bf16[2,16,4608]{2,1,0:T(8,128)(2,1)S(1)} %pad_maximum_fusion) | data formatting | bytes 589824 | tf_op jit(solution)/shard_map/stack | solution.py:34
  11.2 2.5 %reshape.30 = bf16[2,2,36864]{2,1,0:T(2,128)(2,1)S(1)} reshape(bf16[4608,2,16]{2,1,0:T(2,128)(2,1)S(1)} %bitcast.27) | data formatting | bytes 589824
  13.7 9.5 %all_to_all.15 = bf16[2,2,36864]{2,1,0:T(2,128)(2,1)S(1)} all-to-all(bf16[2,2,36864]{2,1,0:T(2,128)(2,1)S(1)} %reshape.30), channel_id=1, replica_groups=mesh['pipe'=4,'dp'=2,'vocab'=4] {'dp'}, dimensions={0} | all-to-all | bytes 589824 | tf_op jit(solution)/shard_map/all_to_all | solution.py:33
  23.3 1.6 reshape.31
  24.9 1.6 copy.32
  26.5 0.2 fusion.6
  26.7 0.7 copy.29
  27.4 0.0 all-gather.4.cloned.1.call-update
  27.4 0.0 copy-start.1
  27.4 0.0 copy-start.2
  27.4 0.0 copy-start.3
  27.4 0.0 reduce-scatter.2.cloned.1.call-start
  27.5 42.7 %all-gather.4.cloned.1.call-done = bf16[512,2304]{1,0:T(8,128)(2,1)} async-done(((bf16[32,2304]{1,0:T(8,128)(2,1)}), bf16[512,2304]{1,0:T(8,128)(2,1)}) %all-gather.4.cloned.1.call-update) | async-done | bytes 2359312 | tf_op jit(solution)/shard_map/all_gather | solution.py:37
  70.2 5.9 %fusion.7 = f32[512,768]{1,0:T(8,128)} fusion(bf16[512,2304]{1,0:T(8,128)(2,1)} %all-gather.4.cloned.1.call-done, bf16[768,2304]{1,0:T(8,128)(2,1)} %param.12), kind=kOutput, calls=%fused_computation.27 | convolution fusion | flops 1811939328 | bytes 7471104 | tf_op jit(solution)/shard_map/dot_general | solution.py:14
  76.0 0.0 copy-start
  76.0 0.0 reduce-scatter.2.cloned.1.call-update
  76.1 0.0 all-gather.6.cloned.1.call-start
  76.1 0.7 copy.31
  76.8 0.0 all-gather.6.cloned.1.call-update
  76.8 0.0 copy-done.1
  76.9 0.0 copy-done.2
  76.9 0.0 copy-done.3
  76.9 66.4 %all-gather = s32[32,16,2]{1,2,0:T(2,128)S(1)} all-gather(s32[1,16,2]{1,2,0:T(2,128)S(1)} %add_bitcast_fusion), channel_id=1, replica_groups=mesh['pipe'=4,'dp'=2,'vocab'=4] {'pipe','vocab','dp'}, dimensions={0}, use_global_device_ids=true | all-gather | bytes 4224 | tf_op jit(solution)/shard_map/all_gather | solution.py:36
  143.3 0.1 reshape.29
  143.4 0.0 reduce-scatter.2.cloned.1.call-done
  143.4 1.6 fusion.4
  145.1 36.9 %psum.7 = f32[2,512]{1,0:T(2,128)S(1)} all-reduce(f32[2,512]{1,0:T(2,128)S(1)} %maximum_dynamic-update-slice_fusion), channel_id=1, replica_groups=mesh['pipe'=4,'dp'=2,'vocab'=4] {'pipe','dp','vocab'}, use_global_device_ids=true, to_apply=%region_3.0 | all-reduce | flops 1024 | bytes 8192 | tf_op jit(solution)/shard_map/psum | solution.py:51
  182.0 0.6 fusion.5
  182.6 1.5 multiply_convert_fusion
  184.1 11.2 %all_gather.14 = bf16[512,768]{1,0:T(8,128)(2,1)S(1)} all-gather(bf16[256,768]{1,0:T(8,128)(2,1)S(1)} %multiply_convert_fusion), channel_id=1, replica_groups=mesh['pipe'=4,'dp'=2,'vocab'=4] {'dp'}, dimensions={0}, use_global_device_ids=true | all-gather | bytes 1179648 | tf_op jit(solution)/shard_map/all_gather | solution.py:56
  195.3 0.0 copy-done
  195.3 5.0 %fusion.8 = f32[768,2304]{1,0:T(8,128)} fusion(bf16[512,768]{1,0:T(8,128)(2,1)S(1)} %all_gather.14, bf16[512,2304]{1,0:T(8,128)(2,1)S(1)} %copy-done), kind=kOutput, calls=%fused_computation.28 | convolution fusion | flops 1811939328 | bytes 10223616 | tf_op jit(solution)/shard_map/dot_general | solution.py:20
  200.3 0.0 all-gather.6.cloned.1.call-done
  200.3 20.3 %broadcast_select_fusion = (bf16[768,2304]{1,0:T(8,128)(2,1)}, bf16[768,2304]{1,0:T(8,128)(2,1)}, bf16[768,2304]{1,0:T(8,128)(2,1)}) fusion(bf16[768,2304]{1,0:T(8,128)(2,1)} %param.15, pred[768]{0:T(1024)(128)(4,1)S(1)} %broadcast_compare_fusion, bf16[768,2304]{1,0:T(8,128)(2,1)} %param.12, bf16[768,2304]{1,0:T(8,128)(2,1)} %param.14, ...), kind=kOutput, calls=%fused_computation.7 | convolution fusion | flops 1858338816 | bytes 30673664 | tf_op jit(solution)/shard_map/dot_general | solution.py:58
  (9 shorter events, 0.1 us)
Async XLA Ops:
  7.2 63.0 %all-gather.4.cloned.1.call-start = ((), (), s32[]{:S(2)}) async-start(), calls=%async_computation.2 | async-start | bytes 2506752 | tf_op jit(solution)/shard_map/all_gather | solution.py:37
  27.4 49.4 %copy-start.1 = (s32[768]{0:T(1024)S(1)}, s32[768]{0:T(1024)}, u32[]{:S(2)}) copy-start(s32[768]{0:T(1024)} %param.13) | copy-start | bytes 9220
  27.4 49.4 %copy-start.2 = (s32[16]{0:T(128)S(1)}, s32[16]{0:T(128)}, u32[]{:S(2)}) copy-start(s32[16]{0:T(128)} %param.10) | copy-start | bytes 196
  27.4 49.4 %copy-start.3 = (s32[16]{0:T(128)S(1)}, s32[16]{0:T(128)}, u32[]{:S(2)}) copy-start(s32[16]{0:T(128)} %param.9) | copy-start | bytes 196
  27.4 116.0 %reduce-scatter.2.cloned.1.call-start = ((), (), s32[]{:S(2)}) async-start(), calls=%async_computation.3 | async-start | bytes 2359296 | tf_op jit(solution)/shard_map/reduce_scatter | solution.py:43
  76.0 119.3 %copy-start = (bf16[512,2304]{1,0:T(8,128)(2,1)S(1)}, bf16[512,2304]{1,0:T(8,128)(2,1)}, u32[]{:S(2)}) copy-start(bf16[512,2304]{1,0:T(8,128)(2,1)} %all-gather.4.cloned.1.call-done) | copy-start | bytes 7077892
  76.1 124.2 %all-gather.6.cloned.1.call-start = ((), (), s32[]{:S(2)}) async-start(), calls=%async_computation.4 | async-start | bytes 2506752 | tf_op jit(solution)/shard_map/all_gather | solution.py:38
Sparse Core Ops, SparseCore 0:
  27.5 42.5 all-gather.3
  76.2 25.0 reduce-scatter.1
  104.4 42.2 all-gather.5

commit v2 on v1

v2 whole, which is shorter than its diff:
```python
import functools
import math

import jax
import jax.numpy as jnp
from jax import lax
from jax.experimental import pallas as pl
from jax.experimental.pallas import tpu as pltpu
from jax.sharding import PartitionSpec as P

SOFTCAP = 30.0
LEARN = 0.01
EPSILON = 1e-08
MESH = pl.DeviceIdType.MESH
CHUNK = 256
VMEM_LIMIT = 56 * 2**20


def chunk_rows(c):
    return pl.ds(c * CHUNK, CHUNK)


class Gather:
    def __init__(self, place, buf, stage, y_send, y_recv, send, recv):
        self.n_pipe, self.n_vocab, self.pipe, self.dp, self.vocab = place
        self.n_x = self.n_pipe // 2
        self.x, self.core = self.pipe // 2, self.pipe % 2
        self.buf, self.stage = buf, stage
        self.y_send, self.y_recv, self.send, self.recv = y_send, y_recv, send, recv
        self.rows = stage.shape[0]
        self.started = []

    def pipe_of(self, k):
        return ((self.x + k) % self.n_x) * 2 + self.core

    def origin(self, k):
        return ((self.x + self.n_x - k) % self.n_x) * 2 + self.core

    def vocab_of(self, k):
        return (self.vocab + k) % self.n_vocab

    def vocab_origin(self, k):
        return (self.vocab + self.n_vocab - k) % self.n_vocab

    def sibling(self):
        return self.pipe + 1 - 2 * self.core

    def own(self, dp):
        block = self.pipe * self.n_vocab + self.vocab
        return pl.ds(pl.multiple_of((block * 2 + dp) * self.rows, self.rows), self.rows)

    def copy(self, pipe, vocab, slot, dest, device):
        block = pipe * self.n_vocab + vocab
        size = 2 * self.rows
        part = self.buf.at[pl.ds(pl.multiple_of(block * size, size), size)]
        return pltpu.make_async_remote_copy(
            src_ref=part, dst_ref=part,
            send_sem=self.send.at[slot, dest], recv_sem=self.recv.at[block],
            device_id=device, device_id_type=MESH,
        )

    def start(self, pipe, vocab, slot, dest, device):
        copy = self.copy(pipe, vocab, slot, dest, device)
        copy.start()
        self.started.append(copy)

    def pair_copy(self):
        return pltpu.make_async_remote_copy(
            src_ref=self.stage, dst_ref=self.buf.at[self.own(self.dp)],
            send_sem=self.y_send, recv_sem=self.y_recv,
            device_id={"dp": 1 - self.dp}, device_id_type=MESH,
        )

    def pair(self):
        copy = self.pair_copy()
        copy.start()
        self.first = copy

    def to_x(self, pipe, vocab, slot):
        for k in range(1, self.n_x):
            self.start(pipe, vocab, slot, self.n_vocab - 2 + k, {"pipe": self.pipe_of(k)})

    def to_core(self, pipe, vocab, slot):
        dest = self.n_vocab + self.n_x - 2
        self.start(pipe, vocab, slot, dest, {"pipe": self.sibling()})

    def arrived(self, pipe, vocab):
        self.copy(pipe, vocab, 0, 0, {"pipe": self.sibling()}).wait_recv()

    def spread(self):
        self.first.wait_recv()
        self.to_x(self.pipe, self.vocab, 0)
        for k in range(1, self.n_vocab):
            self.start(self.pipe, self.vocab, 0, k - 1, {"vocab": self.vocab_of(k)})
        self.to_core(self.pipe, self.vocab, 0)

    def relay(self):
        for k in range(1, self.n_vocab):
            source = self.vocab_origin(k)
            self.arrived(self.pipe, source)
            self.to_x(self.pipe, source, k)
            self.to_core(self.pipe, source, k)
        for j in range(1, self.n_x):
            for k in range(self.n_vocab):
                pipe, source = self.origin(j), self.vocab_origin(k)
                self.arrived(pipe, source)
                self.to_core(pipe, source, j * self.n_vocab + k)

    def finish(self):
        for j in range(self.n_x):
            for k in range(self.n_vocab):
                pipe = self.origin(j) + 1 - 2 * self.core
                self.arrived(pipe, self.vocab_origin(k))

    def sent(self):
        self.first.wait_send()
        for copy in self.started:
            copy.wait_send()


def head_kernel(
    n_pipe, n_vocab, hid, grd, meta, keep, table_hbm,
    hbuf, gbuf, dlog, ids, loss,
    table, hstage, gstage, goals, outgoing, incoming, logits, v_sum, x_sum, c_sum, losses,
    table_sem, hy_send, hy_recv, h_send, h_recv, gy_send, gy_recv, g_send, g_recv,
    l_send, l_recv, d_send, d_recv, vs_send, vs_recv, xs_send, xs_recv, one_send, one_recv,
):
    pipe, dp, vocab = lax.axis_index("pipe"), lax.axis_index("dp"), lax.axis_index("vocab")
    place = (n_pipe, n_vocab, pipe, dp, vocab)
    other = 1 - dp
    vr, half = table.shape
    share = outgoing.shape[1]
    chunks = vr // CHUNK
    row_start = (pipe * n_vocab + vocab) * vr

    load = pltpu.make_async_copy(table_hbm, table, table_sem)
    load.start()
    h = Gather(place, hbuf, hstage, hy_send, hy_recv, h_send, h_recv)
    g = Gather(place, gbuf, gstage, gy_send, gy_recv, g_send, g_recv)

    barrier = pltpu.get_barrier_semaphore()
    peers = [{"dp": other}, {"pipe": h.sibling()}]
    peers += [{"vocab": h.vocab_of(k)} for k in range(1, n_vocab)]
    peers += [{"pipe": h.pipe_of(k)} for k in range(1, h.n_x)]
    for peer in peers:
        pl.semaphore_signal(barrier, inc=1, device_id=peer, device_id_type=MESH)

    mine = pl.ds(pl.multiple_of(dp * half, 128), half)
    theirs = pl.ds(pl.multiple_of(other * half, 128), half)
    hstage[:, :half] = hid[:, theirs]
    hstage[:, half:] = meta[...]
    hbuf[h.own(dp), :half] = hid[:, mine]
    hbuf[h.own(dp), half:] = meta[...]
    gstage[...] = grd[:, theirs]
    gbuf[g.own(dp), :] = grd[:, mine]
    pl.semaphore_wait(barrier, len(peers))

    h.pair()
    g.pair()
    h.spread()
    h.relay()
    h.finish()
    g.spread()

    spots = hbuf[:, half:].astype(jnp.float32).T
    goals[...] = jnp.broadcast_to(
        (spots[0:1] * 256.0 + spots[1:2]).astype(jnp.int32) - row_start, goals.shape
    )
    ids[...] = jnp.broadcast_to(
        (spots[2:3] * 256.0 + spots[3:4]).astype(jnp.int32) - row_start, ids.shape
    )
    load.wait()

    def partial(c, which):
        tokens = pl.ds(pl.multiple_of(which * share, share), share)
        return lax.dot_general(
            table[chunk_rows(c), :], hbuf[tokens, :half],
            (((1,), (1,)), ((), ())), preferred_element_type=jnp.float32,
        )

    def exchange(source, dest, send_sem, recv_sem, device):
        return pltpu.make_async_remote_copy(
            src_ref=source, dst_ref=dest, send_sem=send_sem, recv_sem=recv_sem,
            device_id=device, device_id_type=MESH,
        )

    logit_copies = []
    for c in range(chunks):
        outgoing[chunk_rows(c), :] = partial(c, other)
        copy = exchange(
            outgoing.at[chunk_rows(c)], incoming.at[chunk_rows(c)],
            l_send.at[c], l_recv.at[c], {"dp": other},
        )
        copy.start()
        logit_copies.append(copy)
    for c in range(chunks):
        logits[chunk_rows(c), :] = partial(c, dp)
    g.relay()

    goal = goals[0:1, pl.ds(pl.multiple_of(dp * share, share), share)]
    row_iota = lax.broadcasted_iota(jnp.int32, (CHUNK, share), 0)
    total = jnp.zeros((1, share), jnp.float32)
    target = jnp.zeros((1, share), jnp.float32)
    for c in range(chunks):
        logit_copies[c].wait_recv()
        rows = chunk_rows(c)
        unit = jnp.tanh((logits[rows, :] + incoming[rows, :]) * (1.0 / SOFTCAP))
        capped = SOFTCAP * unit
        weights = jnp.exp(capped) * keep[rows, :]
        hit = row_iota == goal - c * CHUNK
        total += jnp.sum(weights, axis=0, keepdims=True)
        target += jnp.sum(jnp.where(hit, capped, 0.0), axis=0, keepdims=True)
        logits[rows, :] = unit
        incoming[rows, :] = weights

    small = []

    def summed(slots, index, count, offsets, peer, send, recv):
        for k in offsets:
            copy = exchange(slots.at[index], slots.at[index], send.at[k], recv.at[index], peer(k))
            copy.start()
            small.append(copy)
        for k in offsets:
            source = (index + count - k) % count
            exchange(
                slots.at[source], slots.at[source], send.at[k], recv.at[source], peer(k)
            ).wait_recv()
        value = slots[0]
        for k in range(1, count):
            value = value + slots[k]
        return value

    v_sum[vocab, 0:1] = total
    v_sum[vocab, 1:2] = target
    v_sum[vocab, 2:8] = jnp.zeros((6, share), jnp.float32)
    x_sum[h.x] = summed(
        v_sum, vocab, n_vocab, range(1, n_vocab),
        lambda k: {"vocab": h.vocab_of(k)}, vs_send, vs_recv,
    )
    c_sum[h.core] = summed(
        x_sum, h.x, h.n_x, range(1, h.n_x),
        lambda k: {"pipe": h.pipe_of(k)}, xs_send, xs_recv,
    )
    sums = summed(
        c_sum, h.core, 2, range(1, 2),
        lambda k: {"pipe": h.sibling()}, one_send, one_recv,
    )
    total, target = sums[0:1], sums[1:2]
    inverse = 1.0 / total
    dlogit_copies = []
    for c in range(chunks):
        rows = chunk_rows(c)
        unit = logits[rows, :]
        hit = row_iota == goal - c * CHUNK
        slope = 1.0 - unit * unit
        value = (incoming[rows, :] * inverse - jnp.where(hit, 1.0, 0.0)) * slope
        dlog[dp, rows, :] = value.astype(jnp.bfloat16)
        part = dlog.at[dp, rows]
        copy = exchange(part, part, d_send.at[c], d_recv.at[c], {"dp": other})
        copy.start()
        dlogit_copies.append(copy)
    piece = jnp.sum(jnp.log(total) - target, axis=1, keepdims=True)
    losses[dp] = jnp.broadcast_to(piece, losses.shape[1:])
    part = losses.at[dp]
    copy = exchange(part, part, one_send.at[2], one_recv.at[2], {"dp": other})
    copy.start()
    g.finish()
    copy.wait()
    loss[...] = losses[0] + losses[1]
    for copy in dlogit_copies:
        copy.wait()
    for copy in logit_copies + small:
        copy.wait_send()
    h.sent()
    g.sent()


def adam_kernel(scale, dlog, tokens, grads, ids, keep, table, first, second, *outs):
    new_table, new_first, new_second = outs
    rows, width = table.shape
    share = dlog.shape[2]
    row_iota = lax.broadcasted_iota(jnp.int32, (rows, ids.shape[1]), 0)
    here = row_iota + pl.program_id(0) * rows
    selector = jnp.where(ids[0:1, :] == here, 1.0, 0.0).astype(jnp.bfloat16)
    kept = keep[...] > 0.0
    corr_one = 1.0 - 0.9**10
    corr_two = 1.0 - 0.95**10
    step = math.gcd(width, 768)
    for at in range(0, width, step):
        cols = slice(at, at + step)
        grad = scale * jnp.dot(selector, grads[:, cols], preferred_element_type=jnp.float32)
        for j in range(2):
            grad += jnp.dot(
                dlog[j], tokens[j * share:(j + 1) * share, cols],
                preferred_element_type=jnp.float32,
            )
        m1, m2, old = first[:, cols], second[:, cols], table[:, cols]
        f_new = (0.9 * m1.astype(jnp.float32) + 0.1 * grad).astype(jnp.bfloat16)
        s_new = (0.95 * m2.astype(jnp.float32) + 0.05 * grad * grad).astype(jnp.bfloat16)
        root = jnp.sqrt(s_new.astype(jnp.float32) * (1.0 / corr_two)) + EPSILON
        update = f_new.astype(jnp.float32) * (LEARN / corr_one) / root
        t_new = (old.astype(jnp.float32) - update).astype(jnp.bfloat16)
        new_table[:, cols] = jnp.where(kept, t_new, old)
        new_first[:, cols] = jnp.where(kept, f_new, m1)
        new_second[:, cols] = jnp.where(kept, s_new, m2)


def body(hidden, targets, input_ids, input_grads, table, keep, first_moment, second_moment):
    n_pipe, n_vocab = lax.axis_size("pipe"), lax.axis_size("vocab")
    n_x = n_pipe // 2
    here, width = hidden.shape
    vr, half = table.shape
    count = here * 2 * n_pipe * n_vocab
    share = count // 2
    chunks = vr // CHUNK
    meta = jnp.stack(
        [targets // 256, targets % 256, input_ids // 256, input_ids % 256], axis=1
    ).astype(jnp.bfloat16)
    meta = jnp.pad(meta, ((0, 0), (0, 124)))
    keep_col = keep.astype(jnp.float32)[:, None]
    bf16, f32 = jnp.bfloat16, jnp.float32
    vmem = pl.BlockSpec(memory_space=pltpu.VMEM)
    dma = pltpu.SemaphoreType.DMA
    dests = n_vocab + n_x - 1
    tokens, grads, dlog, ids, loss = pl.pallas_call(
        functools.partial(head_kernel, n_pipe, n_vocab),
        out_shape=(
            jax.ShapeDtypeStruct((count, half + 128), bf16),
            jax.ShapeDtypeStruct((count, half), bf16),
            jax.ShapeDtypeStruct((2, vr, share), bf16),
            jax.ShapeDtypeStruct((8, count), jnp.int32),
            jax.ShapeDtypeStruct((8, 128), f32),
        ),
        in_specs=[vmem] * 4 + [pl.BlockSpec(memory_space=pl.ANY)],
        out_specs=(vmem,) * 5,
        scratch_shapes=[
            pltpu.VMEM((vr, half), bf16),
            pltpu.VMEM((here, half + 128), bf16),
            pltpu.VMEM((here, half), bf16),
            pltpu.VMEM((8, count), jnp.int32),
            pltpu.VMEM((vr, share), f32),
            pltpu.VMEM((vr, share), f32),
            pltpu.VMEM((vr, share), f32),
            pltpu.VMEM((n_vocab, 8, share), f32),
            pltpu.VMEM((n_x, 8, share), f32),
            pltpu.VMEM((2, 8, share), f32),
            pltpu.VMEM((2, 8, 128), f32),
            dma,
            dma, dma, dma((n_x * n_vocab, dests)), dma((n_pipe * n_vocab,)),
            dma, dma, dma((n_x * n_vocab, dests)), dma((n_pipe * n_vocab,)),
            dma((chunks,)), dma((chunks,)), dma((chunks,)), dma((chunks,)),
            dma((n_vocab,)), dma((n_vocab,)), dma((n_x,)), dma((n_x,)), dma((3,)), dma((3,)),
        ],
        compiler_params=pltpu.CompilerParams(
            collective_id=0, has_side_effects=True, vmem_limit_bytes=VMEM_LIMIT
        ),
        cost_estimate=pl.CostEstimate(
            flops=2 * count * vr * half, bytes_accessed=2 * vr * half, transcendentals=0
        ),
    )(hidden, input_grads, meta, keep_col, table)

    once = pl.Buffered(buffer_count=1)
    tile = pl.BlockSpec((CHUNK, half), lambda i: (i, 0))
    new_table, new_first, new_second = pl.pallas_call(
        functools.partial(adam_kernel, math.sqrt(width)),
        out_shape=(jax.ShapeDtypeStruct((vr, half), bf16),) * 3,
        grid=(chunks,),
        in_specs=[
            pl.BlockSpec((2, CHUNK, share), lambda i: (0, i, 0)),
            pl.BlockSpec((count, half), lambda i: (0, 0), pipeline_mode=once),
            pl.BlockSpec((count, half), lambda i: (0, 0), pipeline_mode=once),
            pl.BlockSpec((8, count), lambda i: (0, 0)),
            pl.BlockSpec((CHUNK, 1), lambda i: (i, 0)),
            tile, tile, tile,
        ],
        out_specs=(tile,) * 3,
        compiler_params=pltpu.CompilerParams(vmem_limit_bytes=VMEM_LIMIT),
        cost_estimate=pl.CostEstimate(
            flops=4 * count * vr * half, bytes_accessed=12 * vr * half, transcendentals=0
        ),
    )(dlog, tokens, grads, ids, keep_col, table, first_moment, second_moment)
    return (new_table, new_first, new_second, loss[0, 0])


def solution(mesh):
    placed = (
        P(("pipe", "dp", "vocab"), None),
        P(("pipe", "dp", "vocab")),
        P(("pipe", "dp", "vocab")),
        P(("pipe", "dp", "vocab"), None),
        P(("pipe", "vocab"), "dp"),
        P(("pipe", "vocab")),
        P(("pipe", "vocab"), "dp"),
        P(("pipe", "vocab"), "dp"),
    )
    return jax.shard_map(
        body,
        mesh=mesh,
        in_specs=placed,
        out_specs=(
            P(("pipe", "vocab"), "dp"),
            P(("pipe", "vocab"), "dp"),
            P(("pipe", "vocab"), "dp"),
            P(),
        ),
        check_vma=False,
    )
```

time: 228 us -> 93.2 us (0.41)
  blocking collectives: 124 us -> 0 us
  Pallas kernels: 0 us -> 88.1 us
  waiting for transfers between devices: 42.8 us -> 0 us
  matrix products: 31.1 us -> 0 us
  between operations: 13.9 us -> 0.65 us
  local copies, waits for them, and re-layouts: 10.4 us -> 2.81 us
  other arithmetic: 4.81 us -> 1.39 us
    pallas_call x0 -> x2, Pallas kernels: none -> 88.1 us  [the longest x1 72.2 us: body(): pl.pallas_call(functools.partial(head_kernel, n_pipe, n_vocab), out_shape...]
    all_gather x2 -> x0, blocking collectives: 77.6 us -> none  [the longest x1 66.4 us: body(): ids_all = lax.all_gather(both, ('pipe', 'vocab', 'dp'), axis=1, tiled=True)]
    all_gather x2 -> x0, waiting for transfers between devices: 42.7 us -> none  [the longest x1 42.7 us: body(): lax.all_gather(packed[0], ('pipe', 'vocab'), axis=0, tiled=True)]
    psum x1 -> x0, blocking collectives: 36.9 us -> none  [body(): sums = lax.psum(placed, ('pipe', 'dp', 'vocab'))]
    dot_general x3 -> x0, matrix products: 31.1 us -> none  [the longest x1 20.3 us: body(): jnp.dot(selector, grads_all, preferred_element_type=jnp.float32)]
    all_to_all x1 -> x0, blocking collectives: 9.55 us -> none  [body(): lax.all_to_all(jnp.stack([hidden, input_grads]), 'dp', split_axis=2, conc...]
    unnamed x11 -> x0, local copies, waits for them, and re-layouts: 4.16 us -> none
    another operation x1, local copies, waits for them, and re-layouts: 3.01 us -> 0.1 us  [body(): jnp.stack([targets // 256, targets % 256, input_ids // 256, input_ids % 2...]
  transfers between devices with their start and end apart: 3 -> 0, of which waited for: 1 -> 0; matrix products, arithmetic and copies ran while one was open for 4% -> 0% of each run, Pallas kernels for 0% -> 0%
where the time goes in v2:
time: 93.2 us; the launch traced here: 92.9 us
  Pallas kernels  88.1 us (95%)
  local copies, waits for them, and re-layouts  2.81 us (3%)
  other arithmetic  1.39 us (1%)
    pallas_call x1, Pallas kernels, body(): pl.pallas_call(functools.partial(head_kernel, n_pipe, n_vocab), out_shape...  72.2 us
    pallas_call x1, Pallas kernels, body(): pl.pallas_call(functools.partial(adam_kernel, math.sqrt(width)), out_shap...  15.9 us

profile of v2, /device:TPU:0, one launch (start us, length us, event | category | flops | bytes accessed | tf_op | source)
XLA Modules:
  0.0 92.9 jit_solution(16522982141872849784)
XLA Ops:
  0.6 0.7 convert_bitcast_fusion
  1.3 0.1 copy.22
  1.4 0.6 pad.4.meta
  2.0 0.7 convert_element_type.6
  2.7 0.9 broadcast_in_dim.4.keep
  3.7 72.2 %shard_map.111 = (bf16[512,2432]{1,0:T(8,128)(2,1)}, bf16[512,2304]{1,0:T(8,128)(2,1)}, bf16[2,768,256]{2,1,0:T(8,128)(2,1)}, s32[8,512]{1,0:T(8,128)}, f32[8,128]{1,0:T(8,128)}) custom-call(bf16[16,4608]{1,0:T(8,128)(2,1)} %hid.1, bf16[16,4608]{1,0:T(8,128)(2,1)} %grd.1, bf16[16,128]{1,0:T(8,128)(2,1)} %pad.4.meta, f32[768,1]{1,0:T(8,128)} %broadcast_in_dim.4.keep, ...), custom_call_target="tpu_custom_call" | custom-call | flops 1811939328 | bytes 3538944 | tf_op jit(solution)/shard_map/pallas_call | solution.py:325
  75.9 1.2 %slice.3 = f32[1,1]{1,0:T(1,128)} slice(f32[8,128]{1,0:T(8,128)} %get-tuple-element.19), slice={[0:1], [0:1]} | slice | bytes 8 | tf_op jit(solution)/shard_map/slice | solution.py:382
  77.0 15.9 %shard_map.112 = (bf16[768,2304]{1,0:T(8,128)(2,1)}, bf16[768,2304]{1,0:T(8,128)(2,1)}, bf16[768,2304]{1,0:T(8,128)(2,1)}) custom-call(bf16[2,768,256]{2,1,0:T(8,128)(2,1)} %get-tuple-element.12.dlog, bf16[512,2432]{1,0:T(8,128)(2,1)} %get-tuple-element.13.tokens, bf16[512,2304]{1,0:T(8,128)(2,1)} %get-tuple-element.14.grads, ...), custom_call_target="tpu_custom_call" | custom-call | flops 3623878656 | bytes 21233664 | tf_op jit(solution)/shard_map/pallas_call | solution.py:364
  (1 shorter events, 0.0 us)

commit v3 on v2

--- a/solution.py
+++ b/solution.py
@@ -18,6 +18,27 @@
 
 def chunk_rows(c):
     return pl.ds(c * CHUNK, CHUNK)
+
+
+def row_to_column(row):
+    wide = jnp.broadcast_to(row[...].astype(jnp.float32), (8, row.shape[1]))
+    return wide.T[:, 0:1]
+
+
+def id_columns(targets, input_ids):
+    count = targets.shape[1]
+    square = lax.broadcasted_iota(jnp.int32, (count, count), 0) == lax.broadcasted_iota(
+        jnp.int32, (count, count), 1
+    )
+    lane = lax.broadcasted_iota(jnp.int32, (count, 128), 1)
+    result = jnp.zeros((count, 128), jnp.float32)
+    rows = [targets[...] >> 8, targets[...] & 255, input_ids[...] >> 8, input_ids[...] & 255]
+    for at, row in enumerate(rows):
+        column = jnp.sum(
+            jnp.where(square, row.astype(jnp.float32), 0.0), axis=1, keepdims=True
+        )
+        result = jnp.where(lane == at, column, result)
+    return result.astype(jnp.bfloat16)
 
 
 class Gather:
@@ -45,12 +66,15 @@
     def sibling(self):
         return self.pipe + 1 - 2 * self.core
 
+    def block(self, pipe, vocab):
+        return (pipe % 2 * self.n_x + pipe // 2) * self.n_vocab + vocab
+
     def own(self, dp):
-        block = self.pipe * self.n_vocab + self.vocab
+        block = self.block(self.pipe, self.vocab)
         return pl.ds(pl.multiple_of((block * 2 + dp) * self.rows, self.rows), self.rows)
 
     def copy(self, pipe, vocab, slot, dest, device):
-        block = pipe * self.n_vocab + vocab
+        block = self.block(pipe, vocab)
         size = 2 * self.rows
         part = self.buf.at[pl.ds(pl.multiple_of(block * size, size), size)]
         return pltpu.make_async_remote_copy(
@@ -94,23 +118,23 @@
             self.start(self.pipe, self.vocab, 0, k - 1, {"vocab": self.vocab_of(k)})
         self.to_core(self.pipe, self.vocab, 0)
 
-    def relay(self):
+    def relay_near(self):
         for k in range(1, self.n_vocab):
             source = self.vocab_origin(k)
             self.arrived(self.pipe, source)
             self.to_x(self.pipe, source, k)
             self.to_core(self.pipe, source, k)
-        for j in range(1, self.n_x):
-            for k in range(self.n_vocab):
-                pipe, source = self.origin(j), self.vocab_origin(k)
-                self.arrived(pipe, source)
-                self.to_core(pipe, source, j * self.n_vocab + k)
-
-    def finish(self):
-        for j in range(self.n_x):
-            for k in range(self.n_vocab):
-                pipe = self.origin(j) + 1 - 2 * self.core
-                self.arrived(pipe, self.vocab_origin(k))
+
+    def relay_far(self, j):
+        for k in range(self.n_vocab):
+            pipe, source = self.origin(j), self.vocab_origin(k)
+            self.arrived(pipe, source)
+            self.to_core(pipe, source, j * self.n_vocab + k)
+
+    def finish(self, j):
+        for k in range(self.n_vocab):
+            pipe = self.origin(j) + 1 - 2 * self.core
+            self.arrived(pipe, self.vocab_origin(k))
 
     def sent(self):
         self.first.wait_send()
@@ -119,9 +143,9 @@
 
 
 def head_kernel(
-    n_pipe, n_vocab, hid, grd, meta, keep, table_hbm,
+    n_pipe, n_vocab, hid, grd, aims, reads, keep_row, table_hbm,
     hbuf, gbuf, dlog, ids, loss,
-    table, hstage, gstage, goals, outgoing, incoming, logits, v_sum, x_sum, c_sum, losses,
+    table, keep, hstage, gstage, goals, outgoing, incoming, logits, v_sum, x_sum, c_sum, losses,
     table_sem, hy_send, hy_recv, h_send, h_recv, gy_send, gy_recv, g_send, g_recv,
     l_send, l_recv, d_send, d_recv, vs_send, vs_recv, xs_send, xs_recv, one_send, one_recv,
 ):
@@ -148,9 +172,10 @@
     mine = pl.ds(pl.multiple_of(dp * half, 128), half)
     theirs = pl.ds(pl.multiple_of(other * half, 128), half)
     hstage[:, :half] = hid[:, theirs]
-    hstage[:, half:] = meta[...]
+    meta = id_columns(aims, reads)
+    hstage[:, half:] = meta
     hbuf[h.own(dp), :half] = hid[:, mine]
-    hbuf[h.own(dp), half:] = meta[...]
+    hbuf[h.own(dp), half:] = meta
     gstage[...] = grd[:, theirs]
     gbuf[g.own(dp), :] = grd[:, mine]
     pl.semaphore_wait(barrier, len(peers))
@@ -158,23 +183,16 @@
     h.pair()
     g.pair()
     h.spread()
-    h.relay()
-    h.finish()
-    g.spread()
-
-    spots = hbuf[:, half:].astype(jnp.float32).T
-    goals[...] = jnp.broadcast_to(
-        (spots[0:1] * 256.0 + spots[1:2]).astype(jnp.int32) - row_start, goals.shape
-    )
-    ids[...] = jnp.broadcast_to(
-        (spots[2:3] * 256.0 + spots[3:4]).astype(jnp.int32) - row_start, ids.shape
-    )
+    keep[...] = row_to_column(keep_row)
+    h.relay_near()
     load.wait()
 
-    def partial(c, which):
-        tokens = pl.ds(pl.multiple_of(which * share, share), share)
+    group = share // h.n_x
+
+    def partial(c, which, x):
+        start = pl.multiple_of(which * share + x * group, group)
         return lax.dot_general(
-            table[chunk_rows(c), :], hbuf[tokens, :half],
+            table[chunk_rows(c), :], hbuf[pl.ds(start, group), :half],
             (((1,), (1,)), ((), ())), preferred_element_type=jnp.float32,
         )
 
@@ -185,25 +203,48 @@
         )
 
     logit_copies = []
-    for c in range(chunks):
-        outgoing[chunk_rows(c), :] = partial(c, other)
-        copy = exchange(
-            outgoing.at[chunk_rows(c)], incoming.at[chunk_rows(c)],
-            l_send.at[c], l_recv.at[c], {"dp": other},
-        )
-        copy.start()
-        logit_copies.append(copy)
-    for c in range(chunks):
-        logits[chunk_rows(c), :] = partial(c, dp)
-    g.relay()
+    for j in range(h.n_x):
+        if j:
+            h.relay_far(j)
+        h.finish(j)
+        if j == h.n_x - 1:
+            g.spread()
+        x = h.origin(j) // 2
+        lanes = pl.ds(pl.multiple_of(x * group, group), group)
+        for c in range(chunks):
+            rows = chunk_rows(c)
+            outgoing[rows, lanes] = partial(c, other, x)
+            copy = exchange(
+                outgoing.at[rows, lanes], incoming.at[rows, lanes],
+                l_send.at[c, x], l_recv.at[c, x], {"dp": other},
+            )
+            copy.start()
+            logit_copies.append(copy)
+        for c in range(chunks):
+            logits[chunk_rows(c), lanes] = partial(c, dp, x)
+    spots = hbuf[:, half:].astype(jnp.float32).T
+    goals[...] = jnp.broadcast_to(
+        (spots[0:1] * 256.0 + spots[1:2]).astype(jnp.int32) - row_start, goals.shape
+    )
+    ids[...] = jnp.broadcast_to(
+        (spots[2:3] * 256.0 + spots[3:4]).astype(jnp.int32) - row_start, ids.shape
+    )
+    g.relay_near()
+    for j in range(1, g.n_x):
+        g.relay_far(j)
 
     goal = goals[0:1, pl.ds(pl.multiple_of(dp * share, share), share)]
     row_iota = lax.broadcasted_iota(jnp.int32, (CHUNK, share), 0)
     total = jnp.zeros((1, share), jnp.float32)
     target = jnp.zeros((1, share), jnp.float32)
     for c in range(chunks):
-        logit_copies[c].wait_recv()
         rows = chunk_rows(c)
+        for x in range(h.n_x):
+            lanes = pl.ds(x * group, group)
+            exchange(
+                outgoing.at[rows, lanes], incoming.at[rows, lanes],
+                l_send.at[c, x], l_recv.at[c, x], {"dp": other},
+            ).wait_recv()
         unit = jnp.tanh((logits[rows, :] + incoming[rows, :]) * (1.0 / SOFTCAP))
         capped = SOFTCAP * unit
         weights = jnp.exp(capped) * keep[rows, :]
@@ -264,9 +305,10 @@
     part = losses.at[dp]
     copy = exchange(part, part, one_send.at[2], one_recv.at[2], {"dp": other})
     copy.start()
-    g.finish()
+    for j in range(g.n_x):
+        g.finish(j)
     copy.wait()
-    loss[...] = losses[0] + losses[1]
+    loss[...] = losses[0, 0:1, 0:1] + losses[1, 0:1, 0:1]
     for copy in dlogit_copies:
         copy.wait()
     for copy in logit_copies + small:
@@ -275,34 +317,40 @@
     g.sent()
 
 
-def adam_kernel(scale, dlog, tokens, grads, ids, keep, table, first, second, *outs):
-    new_table, new_first, new_second = outs
-    rows, width = table.shape
+def adam_kernel(scale, dlog, tokens, grads, ids, keep, table, first, second, *rest):
+    new_table, new_first, new_second, selector, kept_column = rest
     share = dlog.shape[2]
-    row_iota = lax.broadcasted_iota(jnp.int32, (rows, ids.shape[1]), 0)
-    here = row_iota + pl.program_id(0) * rows
-    selector = jnp.where(ids[0:1, :] == here, 1.0, 0.0).astype(jnp.bfloat16)
-    kept = keep[...] > 0.0
+
+    @pl.when(pl.program_id(0) == 0)
+    def _():
+        row_iota = lax.broadcasted_iota(jnp.int32, selector.shape, 0)
+        hit = ids[0:1, :] == row_iota
+        selector[...] = jnp.where(hit, 1.0, 0.0).astype(jnp.bfloat16)
+        kept_column[...] = row_to_column(keep)
+
     corr_one = 1.0 - 0.9**10
     corr_two = 1.0 - 0.95**10
-    step = math.gcd(width, 768)
-    for at in range(0, width, step):
-        cols = slice(at, at + step)
-        grad = scale * jnp.dot(selector, grads[:, cols], preferred_element_type=jnp.float32)
+    for c in range(table.shape[0] // CHUNK):
+        rows = chunk_rows(c)
+        kept = kept_column[rows, :] > 0.0
+        grad = scale * jnp.dot(
+            selector[rows, :], grads[...], preferred_element_type=jnp.float32
+        )
         for j in range(2):
             grad += jnp.dot(
-                dlog[j], tokens[j * share:(j + 1) * share, cols],
+                dlog[j, rows, :], tokens[j * share:(j + 1) * share, :],
                 preferred_element_type=jnp.float32,
             )
-        m1, m2, old = first[:, cols], second[:, cols], table[:, cols]
+        m1, m2, old = first[rows, :], second[rows, :], table[rows, :]
         f_new = (0.9 * m1.astype(jnp.float32) + 0.1 * grad).astype(jnp.bfloat16)
         s_new = (0.95 * m2.astype(jnp.float32) + 0.05 * grad * grad).astype(jnp.bfloat16)
-        root = jnp.sqrt(s_new.astype(jnp.float32) * (1.0 / corr_two)) + EPSILON
+        square = s_new.astype(jnp.float32) * (1.0 / corr_two)
+        root = square * lax.rsqrt(square) + EPSILON
         update = f_new.astype(jnp.float32) * (LEARN / corr_one) / root
         t_new = (old.astype(jnp.float32) - update).astype(jnp.bfloat16)
-        new_table[:, cols] = jnp.where(kept, t_new, old)
-        new_first[:, cols] = jnp.where(kept, f_new, m1)
-        new_second[:, cols] = jnp.where(kept, s_new, m2)
+        new_table[rows, :] = jnp.where(kept, t_new, old)
+        new_first[rows, :] = jnp.where(kept, f_new, m1)
+        new_second[rows, :] = jnp.where(kept, s_new, m2)
 
 
 def body(hidden, targets, input_ids, input_grads, table, keep, first_moment, second_moment):
@@ -313,11 +361,6 @@
     count = here * 2 * n_pipe * n_vocab
     share = count // 2
     chunks = vr // CHUNK
-    meta = jnp.stack(
-        [targets // 256, targets % 256, input_ids // 256, input_ids % 256], axis=1
-    ).astype(jnp.bfloat16)
-    meta = jnp.pad(meta, ((0, 0), (0, 124)))
-    keep_col = keep.astype(jnp.float32)[:, None]
     bf16, f32 = jnp.bfloat16, jnp.float32
     vmem = pl.BlockSpec(memory_space=pltpu.VMEM)
     dma = pltpu.SemaphoreType.DMA
@@ -329,12 +372,13 @@
             jax.ShapeDtypeStruct((count, half), bf16),
             jax.ShapeDtypeStruct((2, vr, share), bf16),
             jax.ShapeDtypeStruct((8, count), jnp.int32),
-            jax.ShapeDtypeStruct((8, 128), f32),
+            jax.ShapeDtypeStruct((1, 1), f32),
         ),
-        in_specs=[vmem] * 4 + [pl.BlockSpec(memory_space=pl.ANY)],
+        in_specs=[vmem] * 5 + [pl.BlockSpec(memory_space=pl.ANY)],
         out_specs=(vmem,) * 5,
         scratch_shapes=[
             pltpu.VMEM((vr, half), bf16),
+            pltpu.VMEM((vr, 1), f32),
             pltpu.VMEM((here, half + 128), bf16),
             pltpu.VMEM((here, half), bf16),
             pltpu.VMEM((8, count), jnp.int32),
@@ -348,7 +392,7 @@
             dma,
             dma, dma, dma((n_x * n_vocab, dests)), dma((n_pipe * n_vocab,)),
             dma, dma, dma((n_x * n_vocab, dests)), dma((n_pipe * n_vocab,)),
-            dma((chunks,)), dma((chunks,)), dma((chunks,)), dma((chunks,)),
+            dma((chunks, n_x)), dma((chunks, n_x)), dma((chunks,)), dma((chunks,)),
             dma((n_vocab,)), dma((n_vocab,)), dma((n_x,)), dma((n_x,)), dma((3,)), dma((3,)),
         ],
         compiler_params=pltpu.CompilerParams(
@@ -357,28 +401,29 @@
         cost_estimate=pl.CostEstimate(
             flops=2 * count * vr * half, bytes_accessed=2 * vr * half, transcendentals=0
         ),
-    )(hidden, input_grads, meta, keep_col, table)
-
-    once = pl.Buffered(buffer_count=1)
-    tile = pl.BlockSpec((CHUNK, half), lambda i: (i, 0))
+    )(hidden, input_grads, targets[None, :], input_ids[None, :], keep[None, :], table)
+
+    step = math.gcd(half, 256)
+    tile = pl.BlockSpec((vr, step), lambda i: (0, i))
+    part = pl.BlockSpec((count, step), lambda i: (0, i))
     new_table, new_first, new_second = pl.pallas_call(
         functools.partial(adam_kernel, math.sqrt(width)),
         out_shape=(jax.ShapeDtypeStruct((vr, half), bf16),) * 3,
-        grid=(chunks,),
+        grid=(half // step,),
         in_specs=[
-            pl.BlockSpec((2, CHUNK, share), lambda i: (0, i, 0)),
-            pl.BlockSpec((count, half), lambda i: (0, 0), pipeline_mode=once),
-            pl.BlockSpec((count, half), lambda i: (0, 0), pipeline_mode=once),
+            pl.BlockSpec((2, vr, share), lambda i: (0, 0, 0)),
+            part, part,
             pl.BlockSpec((8, count), lambda i: (0, 0)),
-            pl.BlockSpec((CHUNK, 1), lambda i: (i, 0)),
+            pl.BlockSpec((1, vr), lambda i: (0, 0)),
             tile, tile, tile,
         ],
         out_specs=(tile,) * 3,
+        scratch_shapes=[pltpu.VMEM((vr, count), bf16), pltpu.VMEM((vr, 1), f32)],
         compiler_params=pltpu.CompilerParams(vmem_limit_bytes=VMEM_LIMIT),
         cost_estimate=pl.CostEstimate(
             flops=4 * count * vr * half, bytes_accessed=12 * vr * half, transcendentals=0
         ),
-    )(dlog, tokens, grads, ids, keep_col, table, first_moment, second_moment)
+    )(dlog, tokens, grads, ids, keep[None, :], table, first_moment, second_moment)
     return (new_table, new_first, new_second, loss[0, 0])
 
 

time: 93.2 us -> 91.9 us (0.986)
  between operations: 0.65 us -> 2.39 us
  local copies, waits for them, and re-layouts: 2.81 us -> 1.28 us
  other arithmetic: 1.39 us -> 0 us
    slice x1 -> x0, local copies, waits for them, and re-layouts: 1.18 us -> none  [body(): return (new_table, new_first, new_second, loss[0, 0])]
where the time goes in v3:
time: 91.9 us; the launch traced here: 91.5 us
  Pallas kernels  87.8 us (96%)
  between operations  2.39 us (3%)
  local copies, waits for them, and re-layouts  1.28 us (1%)
    pallas_call x1, Pallas kernels, body(): pl.pallas_call(functools.partial(head_kernel, n_pipe, n_vocab), out_shape...  71.8 us
    pallas_call x1, Pallas kernels, body(): pl.pallas_call(functools.partial(adam_kernel, math.sqrt(width)), out_shap...  15.9 us

profile of v3, /device:TPU:0, one launch (start us, length us, event | category | flops | bytes accessed | tf_op | source)
XLA Modules:
  0.0 91.5 jit_solution(8675851558427376313)
XLA Ops:
  0.6 1.3 %broadcast_in_dim.12.keep_row.keep = s32[1,768]{1,0:T(1,128)} reshape(s32[768]{0:T(1024)} %param.13) | data formatting | bytes 6144 | tf_op jit(solution)/shard_map/broadcast_in_dim | solution.py:404
  1.9 71.8 %shard_map.111 = (bf16[512,2432]{1,0:T(8,128)(2,1)}, bf16[512,2304]{1,0:T(8,128)(2,1)}, bf16[2,768,256]{2,1,0:T(8,128)(2,1)}, s32[8,512]{1,0:T(8,128)}, f32[1,1]{1,0:T(1,128)}) custom-call(bf16[16,4608]{1,0:T(8,128)(2,1)} %hid.1, bf16[16,4608]{1,0:T(8,128)(2,1)} %grd.1, s32[1,16]{1,0:T(1,128)} %bitcast.3, s32[1,16]{1,0:T(1,128)} %bitcast.4, ...), custom_call_target="tpu_custom_call" | custom-call | flops 1811939328 | bytes 3538944 | tf_op jit(solution)/shard_map/pallas_call | solution.py:368
  73.8 15.9 %shard_map.112 = (bf16[768,2304]{1,0:T(8,128)(2,1)}, bf16[768,2304]{1,0:T(8,128)(2,1)}, bf16[768,2304]{1,0:T(8,128)(2,1)}) custom-call(bf16[2,768,256]{2,1,0:T(8,128)(2,1)} %get-tuple-element.12.dlog, bf16[512,2432]{1,0:T(8,128)(2,1)} %get-tuple-element.13.tokens, bf16[512,2304]{1,0:T(8,128)(2,1)} %get-tuple-element.14.grads, ...), custom_call_target="tpu_custom_call" | custom-call | flops 3623878656 | bytes 21233664 | tf_op jit(solution)/shard_map/pallas_call | solution.py:409

commit v4 on v3

--- a/solution.py
+++ b/solution.py
@@ -49,7 +49,6 @@
         self.buf, self.stage = buf, stage
         self.y_send, self.y_recv, self.send, self.recv = y_send, y_recv, send, recv
         self.rows = stage.shape[0]
-        self.started = []
 
     def pipe_of(self, k):
         return ((self.x + k) % self.n_x) * 2 + self.core
@@ -86,7 +85,6 @@
     def start(self, pipe, vocab, slot, dest, device):
         copy = self.copy(pipe, vocab, slot, dest, device)
         copy.start()
-        self.started.append(copy)
 
     def pair_copy(self):
         return pltpu.make_async_remote_copy(
@@ -102,11 +100,10 @@
 
     def to_x(self, pipe, vocab, slot):
         for k in range(1, self.n_x):
-            self.start(pipe, vocab, slot, self.n_vocab - 2 + k, {"pipe": self.pipe_of(k)})
+            self.start(pipe, vocab, slot, 1 + k, {"pipe": self.pipe_of(k)})
 
     def to_core(self, pipe, vocab, slot):
-        dest = self.n_vocab + self.n_x - 2
-        self.start(pipe, vocab, slot, dest, {"pipe": self.sibling()})
+        self.start(pipe, vocab, slot, self.n_x + 1, {"pipe": self.sibling()})
 
     def arrived(self, pipe, vocab):
         self.copy(pipe, vocab, 0, 0, {"pipe": self.sibling()}).wait_recv()
@@ -114,16 +111,38 @@
     def spread(self):
         self.first.wait_recv()
         self.to_x(self.pipe, self.vocab, 0)
-        for k in range(1, self.n_vocab):
-            self.start(self.pipe, self.vocab, 0, k - 1, {"vocab": self.vocab_of(k)})
+        self.to_right(self.vocab, 0)
+        self.to_left(self.vocab, 0)
         self.to_core(self.pipe, self.vocab, 0)
+
+    def to_right(self, vocab, slot):
+        @pl.when(self.vocab < self.n_vocab - 1)
+        def _():
+            self.start(self.pipe, vocab, slot, 0, {"vocab": self.vocab + 1})
+
+    def to_left(self, vocab, slot):
+        @pl.when(self.vocab > 0)
+        def _():
+            self.start(self.pipe, vocab, slot, 1, {"vocab": self.vocab - 1})
 
     def relay_near(self):
         for k in range(1, self.n_vocab):
-            source = self.vocab_origin(k)
-            self.arrived(self.pipe, source)
-            self.to_x(self.pipe, source, k)
-            self.to_core(self.pipe, source, k)
+
+            @pl.when(self.vocab >= k)
+            def _():
+                source = self.vocab - k
+                self.arrived(self.pipe, source)
+                self.to_right(source, k)
+                self.to_x(self.pipe, source, k)
+                self.to_core(self.pipe, source, k)
+
+            @pl.when(self.vocab + k < self.n_vocab)
+            def _():
+                source, slot = self.vocab + k, self.n_vocab - k
+                self.arrived(self.pipe, source)
+                self.to_left(source, slot)
+                self.to_x(self.pipe, source, slot)
+                self.to_core(self.pipe, source, slot)
 
     def relay_far(self, j):
         for k in range(self.n_vocab):
@@ -138,8 +157,24 @@
 
     def sent(self):
         self.first.wait_send()
-        for copy in self.started:
-            copy.wait_send()
+        for k in range(self.n_vocab):
+
+            @pl.when((self.vocab >= k) & (self.vocab < self.n_vocab - 1))
+            def _():
+                self.sent_one(self.pipe, self.vocab - k, k, 0)
+
+            @pl.when((self.vocab + k < self.n_vocab) & (self.vocab > 0))
+            def _():
+                self.sent_one(self.pipe, self.vocab + k, (self.n_vocab - k) % self.n_vocab, 1)
+
+            source = self.vocab_origin(k)
+            for j in range(1, self.n_x):
+                self.sent_one(self.pipe, source, k, 1 + j)
+            for j in range(self.n_x):
+                self.sent_one(self.origin(j), source, j * self.n_vocab + k, self.n_x + 1)
+
+    def sent_one(self, pipe, vocab, slot, dest):
+        self.copy(pipe, vocab, slot, dest, {"pipe": self.sibling()}).wait_send()
 
 
 def head_kernel(
@@ -181,8 +216,8 @@
     pl.semaphore_wait(barrier, len(peers))
 
     h.pair()
+    h.spread()
     g.pair()
-    h.spread()
     keep[...] = row_to_column(keep_row)
     h.relay_near()
     load.wait()
@@ -364,7 +399,7 @@
     bf16, f32 = jnp.bfloat16, jnp.float32
     vmem = pl.BlockSpec(memory_space=pltpu.VMEM)
     dma = pltpu.SemaphoreType.DMA
-    dests = n_vocab + n_x - 1
+    dests = n_x + 2
     tokens, grads, dlog, ids, loss = pl.pallas_call(
         functools.partial(head_kernel, n_pipe, n_vocab),
         out_shape=(

time: 91.9 us -> 87.8 us (0.955)
  Pallas kernels: 87.8 us -> 83.7 us
    pallas_call x1, Pallas kernels: 71.8 us -> 67.8 us  [body(): pl.pallas_call(functools.partial(head_kernel, n_pipe, n_vocab), out_shape...]
where the time goes in v4:
time: 87.8 us; the launch traced here: 87.4 us
  Pallas kernels  83.7 us (95%)
  between operations  2.39 us (3%)
  local copies, waits for them, and re-layouts  1.28 us (1%)
    pallas_call x1, Pallas kernels, body(): pl.pallas_call(functools.partial(head_kernel, n_pipe, n_vocab), out_shape...  67.8 us
    pallas_call x1, Pallas kernels, body(): pl.pallas_call(functools.partial(adam_kernel, math.sqrt(width)), out_shap...  15.9 us

profile of v4, /device:TPU:0, one launch (start us, length us, event | category | flops | bytes accessed | tf_op | source)
XLA Modules:
  0.0 87.4 jit_solution(12201059738250549261)
XLA Ops:
  0.6 1.3 %broadcast_in_dim.12.keep_row.keep = s32[1,768]{1,0:T(1,128)} reshape(s32[768]{0:T(1024)} %param.13) | data formatting | bytes 6144 | tf_op jit(solution)/shard_map/broadcast_in_dim | solution.py:439
  1.9 67.8 %shard_map.111 = (bf16[512,2432]{1,0:T(8,128)(2,1)}, bf16[512,2304]{1,0:T(8,128)(2,1)}, bf16[2,768,256]{2,1,0:T(8,128)(2,1)}, s32[8,512]{1,0:T(8,128)}, f32[1,1]{1,0:T(1,128)}) custom-call(bf16[16,4608]{1,0:T(8,128)(2,1)} %hid.1, bf16[16,4608]{1,0:T(8,128)(2,1)} %grd.1, s32[1,16]{1,0:T(1,128)} %bitcast.3, s32[1,16]{1,0:T(1,128)} %bitcast.4, ...), custom_call_target="tpu_custom_call" | custom-call | flops 1811939328 | bytes 3538944 | tf_op jit(solution)/shard_map/pallas_call | solution.py:403
  69.7 15.9 %shard_map.112 = (bf16[768,2304]{1,0:T(8,128)(2,1)}, bf16[768,2304]{1,0:T(8,128)(2,1)}, bf16[768,2304]{1,0:T(8,128)(2,1)}) custom-call(bf16[2,768,256]{2,1,0:T(8,128)(2,1)} %get-tuple-element.12.dlog, bf16[512,2432]{1,0:T(8,128)(2,1)} %get-tuple-element.13.tokens, bf16[512,2304]{1,0:T(8,128)(2,1)} %get-tuple-element.14.grads, ...), custom_call_target="tpu_custom_call" | custom-call | flops 3623878656 | bytes 21233664 | tf_op jit(solution)/shard_map/pallas_call | solution.py:444

commit v5 on v4

--- a/solution.py
+++ b/solution.py
@@ -241,9 +241,9 @@
     for j in range(h.n_x):
         if j:
             h.relay_far(j)
-        h.finish(j)
         if j == h.n_x - 1:
             g.spread()
+        h.finish(j)
         x = h.origin(j) // 2
         lanes = pl.ds(pl.multiple_of(x * group, group), group)
         for c in range(chunks):
@@ -365,8 +365,9 @@
 
     corr_one = 1.0 - 0.9**10
     corr_two = 1.0 - 0.95**10
-    for c in range(table.shape[0] // CHUNK):
-        rows = chunk_rows(c)
+    size = CHUNK // 2
+    for c in range(table.shape[0] // size):
+        rows = pl.ds(c * size, size)
         kept = kept_column[rows, :] > 0.0
         grad = scale * jnp.dot(
             selector[rows, :], grads[...], preferred_element_type=jnp.float32

time: 87.8 us -> 85.8 us (0.977)
  Pallas kernels: 83.7 us -> 81.5 us
    pallas_call x1, Pallas kernels: 67.8 us -> 65.7 us  [body(): pl.pallas_call(functools.partial(head_kernel, n_pipe, n_vocab), out_shape...]
where the time goes in v5:
time: 85.8 us; the launch traced here: 85.2 us
  Pallas kernels  81.5 us (95%)
  between operations  2.39 us (3%)
  local copies, waits for them, and re-layouts  1.28 us (1%)
    pallas_call x1, Pallas kernels, body(): pl.pallas_call(functools.partial(head_kernel, n_pipe, n_vocab), out_shape...  65.7 us
    pallas_call x1, Pallas kernels, body(): pl.pallas_call(functools.partial(adam_kernel, math.sqrt(width)), out_shap...  15.8 us

profile of v5, /device:TPU:0, one launch (start us, length us, event | category | flops | bytes accessed | tf_op | source)
XLA Modules:
  0.0 85.2 jit_solution(730809341617301)
XLA Ops:
  0.6 1.3 %broadcast_in_dim.12.keep_row.keep = s32[1,768]{1,0:T(1,128)} reshape(s32[768]{0:T(1024)} %param.13) | data formatting | bytes 6144 | tf_op jit(solution)/shard_map/broadcast_in_dim | solution.py:440
  1.9 65.7 %shard_map.111 = (bf16[512,2432]{1,0:T(8,128)(2,1)}, bf16[512,2304]{1,0:T(8,128)(2,1)}, bf16[2,768,256]{2,1,0:T(8,128)(2,1)}, s32[8,512]{1,0:T(8,128)}, f32[1,1]{1,0:T(1,128)}) custom-call(bf16[16,4608]{1,0:T(8,128)(2,1)} %hid.1, bf16[16,4608]{1,0:T(8,128)(2,1)} %grd.1, s32[1,16]{1,0:T(1,128)} %bitcast.3, s32[1,16]{1,0:T(1,128)} %bitcast.4, ...), custom_call_target="tpu_custom_call" | custom-call | flops 1811939328 | bytes 3538944 | tf_op jit(solution)/shard_map/pallas_call | solution.py:404
  67.6 15.8 %shard_map.112 = (bf16[768,2304]{1,0:T(8,128)(2,1)}, bf16[768,2304]{1,0:T(8,128)(2,1)}, bf16[768,2304]{1,0:T(8,128)(2,1)}) custom-call(bf16[2,768,256]{2,1,0:T(8,128)(2,1)} %get-tuple-element.12.dlog, bf16[512,2432]{1,0:T(8,128)(2,1)} %get-tuple-element.13.tokens, bf16[512,2304]{1,0:T(8,128)(2,1)} %get-tuple-element.14.grads, ...), custom_call_target="tpu_custom_call" | custom-call | flops 3623878656 | bytes 21233664 | tf_op jit(solution)/shard_map/pallas_call | solution.py:445
